TPU v7x, 512 devices: a whole 4x4x16 slice. The times are simulated.
512 devices in a mesh: ctx: 64 (over z, y_lo, core), chan: 8 (over x, y_hi).
Axes of the slice: x: 4, y: 4 (y_hi: 2, y_lo: 2; y = y_hi * 2 + y_lo), z: 16, core: 2. Of those that a mesh axis runs over, the one named last changes fastest.
Arguments:
- query_in: bfloat16 [8192, 1024], P('ctx', 'chan'), may hold values from -6 to 6
- key_in: bfloat16 [8192, 1024], P('ctx', 'chan'), may hold values from -6 to 6
- value_in: bfloat16 [8192, 1024], P('ctx', 'chan'), may hold values from -6 to 6
- grad_out: bfloat16 [8192, 1024], P('ctx', 'chan'), may hold values from -6 to 6
- residue: float32 [16, 1024], P(None, 'chan'), may hold values from -0.34 to 0.34
- decay_rate: float32 [16, 1024], P(None, 'chan'), may hold values from 1.0986328125e-05 to 0.05
Outputs:
- grad_query: bfloat16 [8192, 1024], P('ctx', 'chan')
- grad_key: bfloat16 [8192, 1024], P('ctx', 'chan')
- grad_value: bfloat16 [8192, 1024], P('ctx', 'chan')
- grad_residue: float32 [16, 1024], P(None, 'chan')
- grad_log_rate: float32 [16, 1024], P(None, 'chan')
- filter_norm: float32 [], replicated
All inputs are finite; a program needn't handle non-finite values.
Results may differ from a plain program's by a relative error of at most 0.003.
Values may be sent and summed in bfloat16 or wider, within the bound.
No kernel may reach another device: no remote copies, remote signals or barrier semaphores. Data moves between devices by JAX's collectives and lax.ppermute only.
A program may use at most 64 MiB of HBM per device.

v0:
```python
import jax
import jax.numpy as jnp
from jax import lax
from jax.sharding import PartitionSpec as P


def forward_combine(early, late):
    return (early[0] * late[0], late[0] * early[1] + late[1])


def backward_combine(right, left):
    right_a, right_b, right_g, right_p = right
    left_a, left_b, left_g, left_p = left
    return (
        left_a * right_a,
        left_a * right_b + left_b * right_a,
        left_a * right_g + left_g,
        left_a * right_p + left_b * right_g + left_p,
    )


def tri_product(matrix, values):
    row_count = values.shape[0]
    flat = values.reshape(row_count, -1)
    out = jnp.dot(matrix, flat, preferred_element_type=jnp.float32, precision=lax.Precision.HIGHEST)
    return out.reshape(values.shape)


def sweep(mixed_in, grad_mix, rates, residues, forward_prefix, backward_prefix):
    row_count = mixed_in.shape[0]
    rows_idx = lax.broadcasted_iota(jnp.int32, (row_count, row_count), 0)
    cols_idx = lax.broadcasted_iota(jnp.int32, (row_count, row_count), 1)
    lower = (rows_idx >= cols_idx).astype(jnp.float32)
    upper = (rows_idx <= cols_idx).astype(jnp.float32)
    lagged = upper * (cols_idx - rows_idx).astype(jnp.float32)
    where_at = jnp.arange(row_count, dtype=jnp.float32)[:, None, None]
    grow = jnp.exp(rates[None] * where_at)
    shrink = jnp.exp(-rates[None] * where_at)
    local_x = tri_product(lower, grow * mixed_in[:, None, :]) * shrink
    span = jnp.exp(-rates * row_count)
    entering = forward_prefix((span, local_x[-1]))[1]
    ahead = where_at + 1.0
    states = local_x + jnp.exp(-rates[None] * ahead) * entering[None]
    conv_part = jnp.sum(residues[None] * states, axis=1)
    weighted = shrink * grad_mix[:, None, :]
    local_g = tri_product(upper, weighted) * grow
    local_p = tri_product(lagged, weighted) * grow
    leaving = backward_prefix((span, row_count * span, local_g[0], local_p[0]))
    behind = jnp.arange(row_count, 0, -1, dtype=jnp.float32)[:, None, None]
    reach = jnp.exp(-rates[None] * behind)
    adjoint = local_g + reach * leaving[2][None]
    second = local_p + reach * leaving[3][None] + behind * reach * leaving[2][None]
    grad_part = jnp.sum(residues[None] * adjoint, axis=1)
    res_sum = jnp.sum(mixed_in[:, None, :] * adjoint, axis=0)
    rate_sum = jnp.sum(mixed_in[:, None, :] * second, axis=0)
    return (conv_part, grad_part, res_sum, rate_sum)


def block_prefix(summary, combine, identity, dev_count, reverse):
    pieces = tuple((part.reshape(part.shape[0], dev_count, -1) for part in summary))
    inclusive = lax.associative_scan(combine, pieces, axis=1, reverse=reverse)
    result = []
    for part, unit in zip(inclusive, identity):
        filler = jnp.full((part.shape[0], 1, part.shape[2]), unit, jnp.float32)
        if reverse:
            shifted = jnp.concatenate([part[:, 1:], filler], 1)
        else:
            shifted = jnp.concatenate([filler, part[:, :-1]], 1)
        result.append(shifted.reshape(part.shape[0], -1))
    return tuple(result)


def on_device(query_in, key_in, value_in, grad_out, residue, decay_rate):
    row_count, chan_count = query_in.shape
    dev_count = lax.axis_size("ctx")
    total_rows = row_count * dev_count
    chan_width = chan_count // dev_count
    stacked = jnp.stack([query_in, key_in, value_in, grad_out]).reshape(
        4, row_count, dev_count, chan_width
    )
    moved = lax.all_to_all(stacked, "ctx", split_axis=2, concat_axis=2, tiled=True).reshape(
        4, row_count, chan_count
    )
    start = lax.axis_index("ctx") * chan_width
    res_lanes = jnp.tile(lax.dynamic_slice_in_dim(residue, start, chan_width, 1), (1, dev_count))
    rate_lanes = jnp.tile(
        lax.dynamic_slice_in_dim(decay_rate, start, chan_width, 1), (1, dev_count)
    )

    def forward_prefix(summary):
        return block_prefix(summary, forward_combine, (1.0, 0.0), dev_count, False)

    def backward_prefix(summary):
        return block_prefix(summary, backward_combine, (1.0, 0.0, 0.0, 0.0), dev_count, True)

    query_local = moved[0].astype(jnp.float32)
    key_local = moved[1].astype(jnp.float32)
    value_local = moved[2].astype(jnp.float32)
    grad_local = moved[3].astype(jnp.float32)
    mixed_in = key_local * value_local
    grad_mix = grad_local * query_local
    conv, grad_conv, res_sum, rate_sum = sweep(
        mixed_in, grad_mix, rate_lanes, res_lanes, forward_prefix, backward_prefix
    )
    results = jnp.stack(
        [
            (grad_local * conv).astype(jnp.bfloat16),
            (grad_conv * value_local).astype(jnp.bfloat16),
            (grad_conv * key_local).astype(jnp.bfloat16),
        ]
    )
    results = results.reshape(3, row_count, dev_count, chan_width)
    returned = lax.all_to_all(results, "ctx", split_axis=2, concat_axis=2, tiled=True).reshape(
        3, row_count, chan_count
    )
    grad_query = returned[0]
    grad_key = returned[1]
    grad_value = returned[2]
    res_sum = jnp.sum(res_sum.reshape(res_sum.shape[0], dev_count, chan_width), axis=1)
    rate_sum = jnp.sum(rate_sum.reshape(rate_sum.shape[0], dev_count, chan_width), axis=1)
    res_full, rate_full = (
        lax.all_gather(res_sum, "ctx", axis=1, tiled=True),
        lax.all_gather(rate_sum, "ctx", axis=1, tiled=True),
    )
    grad_residue = res_full / total_rows
    grad_log_rate = -decay_rate * residue * rate_full / total_rows
    squares = jnp.sum(grad_residue * grad_residue + grad_log_rate * grad_log_rate)
    filter_norm = jnp.sqrt(lax.psum(squares, "chan"))
    return (grad_query, grad_key, grad_value, grad_residue, grad_log_rate, filter_norm)


def solution(mesh):
    return jax.shard_map(
        on_device,
        mesh=mesh,
        in_specs=(
            P("ctx", "chan"),
            P("ctx", "chan"),
            P("ctx", "chan"),
            P("ctx", "chan"),
            P(None, "chan"),
            P(None, "chan"),
        ),
        out_specs=(
            P("ctx", "chan"),
            P("ctx", "chan"),
            P("ctx", "chan"),
            P(None, "chan"),
            P(None, "chan"),
            P(),
        ),
        check_vma=False,
    )
```

profile of v0, /device:TPU:1, one launch (start us, length us, event | category | flops | bytes accessed | tf_op | source)
XLA Modules:
  0.0 238.0 jit_solution(15003863092018827185)
XLA Ops:
  0.6 0.9 copy.128
  1.7 0.6 copy-done.14
  2.4 0.6 copy-done.15
  3.4 0.8 copy.129
  4.2 18.3 %all-to-all-start = ((bf16[4,128,64,2]{1,3,0,2:T(2,128)(2,1)}), bf16[4,128,64,2]{1,3,0,2:T(2,128)(2,1)S(1)}, u32[]{:S(2)}, u32[]{:S(2)}) async-start(bf16[4,128,64,2]{1,3,0,2:T(2,128)(2,1)} %copy.129), calls=%async_computation | async-start | bytes 262144 | tf_op jit(solution)/shard_map/all_to_all | solution.py:81
  22.5 0.7 copy-done.17
  25.1 14.5 %all-to-all-done = bf16[4,128,64,2]{1,3,0,2:T(2,128)(2,1)S(1)} async-done(((bf16[4,128,64,2]{1,3,0,2:T(2,128)(2,1)}), bf16[4,128,64,2]{1,3,0,2:T(2,128)(2,1)S(1)}, u32[]{:S(2)}, u32[]{:S(2)}) %all-to-all-start) | async-done | bytes 131104 | tf_op jit(solution)/shard_map/all_to_all | solution.py:81
  40.0 0.8 convolution_multiply_fusion.1
  40.8 1.1 convolution_multiply_fusion
  48.0 0.8 convolution_multiply_fusion.2
  49.0 0.7 copy-done.29
  50.3 0.7 copy-done.34
  51.6 0.7 copy-done.30
  53.1 0.7 slice-done.1
  55.9 5.6 %pad.123 = f32[16,32,2]{0,2,1:T(2,128)S(1)} pad(f32[16,16,2]{0,2,1:T(2,128)} %add.338, f32[]{:T(128)} %constant.24.clone.1), padding=0_0_0x1_0_1x0_0_0 | pad | bytes 6148 | tf_op jit(solution)/shard_map/pad | solution.py:61
  62.0 5.5 %pad.122 = f32[16,32,2]{0,2,1:T(2,128)S(1)} pad(f32[16,16,2]{0,2,1:T(2,128)} %pad_maximum_fusion.5, f32[]{:T(128)} %constant.24.clone.1), padding=0_0_0x0_1_1x0_0_0 | pad | bytes 6148 | tf_op jit(solution)/shard_map/pad | solution.py:61
  72.2 0.7 copy-done.27
  73.0 0.7 fusion.19
  73.7 0.7 copy-done.32
  75.3 0.7 copy.146
  78.0 0.7 copy-done.5
  80.7 1.0 multiply_reduce_fusion.1
  82.1 0.7 copy.148
  82.8 4.4 %all-to-all-start.1 = ((bf16[3,128,64,2]{1,3,0,2:T(2,128)(2,1)}), bf16[3,128,64,2]{1,3,0,2:T(2,128)(2,1)S(1)}, u32[]{:S(2)}, u32[]{:S(2)}) async-start(bf16[3,128,64,2]{1,3,0,2:T(2,128)(2,1)} %copy.148), calls=%async_computation.1 | async-start | bytes 196608 | tf_op jit(solution)/shard_map/all_to_all | solution.py:113
  87.4 63.7 %all-gather = f32[64,2,16]{2,1,0:T(2,128)S(1)} all-gather(f32[1,2,16]{2,1,0:T(2,128)S(1)} %bitcast.122), channel_id=1, replica_groups=mesh['ctx'=64,'chan'=8] {'ctx'}, dimensions={0}, use_global_device_ids=true | all-gather | bytes 8320 | tf_op jit(solution)/shard_map/all_gather | solution.py:122
  151.4 59.6 %all-gather.1 = f32[64,2,16]{2,1,0:T(2,128)S(1)} all-gather(f32[1,2,16]{2,1,0:T(2,128)S(1)} %bitcast.121), channel_id=1, replica_groups=mesh['ctx'=64,'chan'=8] {'ctx'}, dimensions={0}, use_global_device_ids=true | all-gather | bytes 8320 | tf_op jit(solution)/shard_map/all_gather | solution.py:123
  211.1 0.6 copy-done.18
  211.8 1.2 add_reduce_fusion
  213.0 20.9 %psum.7 = f32[]{:T(128)} all-reduce(f32[]{:T(128)} %get-tuple-element.28), channel_id=1, replica_groups=mesh['ctx'=64,'chan'=8] {'chan'}, use_global_device_ids=true, to_apply=%region_7.0 | all-reduce | flops 1 | bytes 8 | tf_op jit(solution)/shard_map/psum | solution.py:128
  234.7 0.7 copy.155
  235.4 0.7 copy.156
  236.1 0.7 copy.157
  (220 shorter events, 24.4 us)
Async XLA Ops:
  0.6 0.9 copy-start.13
  1.5 0.8 copy-start.14
  2.3 0.8 copy-start.15
  4.2 18.3 %copy-start.19 = (f32[16,128]{1,0:T(8,128)S(1)}, f32[16,128]{1,0:T(8,128)}, u32[]{:S(2)}) copy-start(f32[16,128]{1,0:T(8,128)} %param.10) | copy-start | bytes 24580
  4.2 35.4 %all-to-all-start = ((bf16[4,128,64,2]{1,3,0,2:T(2,128)(2,1)}), bf16[4,128,64,2]{1,3,0,2:T(2,128)(2,1)S(1)}, u32[]{:S(2)}, u32[]{:S(2)}) async-start(bf16[4,128,64,2]{1,3,0,2:T(2,128)(2,1)} %copy.129), calls=%async_computation | async-start | bytes 262144 | tf_op jit(solution)/shard_map/all_to_all | solution.py:81
  22.5 0.7 copy-start.17
  25.1 17.1 %copy-start.26 = (f32[16,2]{0,1:T(2,128)}, f32[16,2]{0,1:T(2,128)S(1)}, u32[]{:S(2)}) copy-start(f32[16,2]{0,1:T(2,128)S(1)} %get-tuple-element.86) | copy-start | bytes 388
  25.1 23.8 %copy-start.21 = (f32[16,2]{0,1:T(2,128)}, f32[16,2]{0,1:T(2,128)S(1)}, u32[]{:S(2)}) copy-start(f32[16,2]{0,1:T(2,128)S(1)} %get-tuple-element.89) | copy-start | bytes 388
  25.1 23.8 %copy-start.24 = (f32[16,2]{0,1:T(2,128)}, f32[16,2]{0,1:T(2,128)S(1)}, u32[]{:S(2)}) copy-start(f32[16,2]{0,1:T(2,128)S(1)} %get-tuple-element.85) | copy-start | bytes 388
  48.9 6.4 %copy-start = (f32[16,32,2]{0,2,1:T(2,128)}, f32[16,32,2]{0,2,1:T(2,128)S(1)}, u32[]{:S(2)}) copy-start(f32[16,32,2]{0,2,1:T(2,128)S(1)} %slice_add_fusion) | copy-start | bytes 12292
  49.0 4.1 %copy-start.6 = (f32[16,16,2]{0,2,1:T(2,128)}, f32[16,16,2]{0,2,1:T(2,128)S(1)}, u32[]{:S(2)}) copy-start(f32[16,16,2]{0,2,1:T(2,128)S(1)} %slice_add_fusion.4) | copy-start | bytes 6148
  49.0 0.7 copy-start.29
  49.7 2.7 %copy-start.11 = (f32[16,8,2]{0,2,1:T(2,128)}, f32[16,8,2]{0,2,1:T(2,128)S(1)}, u32[]{:S(2)}) copy-start(f32[16,8,2]{0,2,1:T(2,128)S(1)} %slice_add_fusion.9) | copy-start | bytes 3076
  52.4 0.7 slice-start.2
  53.1 0.7 slice-start.1
  55.9 5.6 %slice-start = ((f32[16,32,2]{0,2,1:T(2,128)}), f32[16,1,2]{0,2,1:T(2,128)S(1)}, s32[]{:S(2)}) async-start(f32[16,32,2]{0,2,1:T(2,128)} %copy-done), calls=%async_computation.2 | async-start | bytes 2048 | tf_op jit(solution)/shard_map/slice | solution.py:61
  55.9 5.6 %copy-start.10 = (f32[16,15,2]{0,2,1:T(2,128)S(1)}, f32[16,15,2]{0,2,1:T(2,128)}, u32[]{:S(2)}) copy-start(f32[16,15,2]{0,2,1:T(2,128)} %fusion.23) | copy-start | bytes 5764
  62.0 5.5 %copy-start.22 = (f32[16,2]{0,1:T(2,128)S(1)}, f32[16,2]{0,1:T(2,128)}, u32[]{:S(2)}) copy-start(f32[16,2]{0,1:T(2,128)} %copy-done.21) | copy-start | bytes 388
  68.9 0.7 copy-start.9
  69.7 0.7 copy-start.7
  70.4 0.7 copy-start.8
  72.2 0.8 copy-start.3
  75.3 0.8 copy-start.4
  76.6 0.8 copy-start.2
  77.9 0.8 copy-start.5
  77.9 0.7 copy-start.33
  78.7 0.8 copy-start.1
  79.9 0.7 copy-start.12
  82.8 151.8 %all-to-all-start.1 = ((bf16[3,128,64,2]{1,3,0,2:T(2,128)(2,1)}), bf16[3,128,64,2]{1,3,0,2:T(2,128)(2,1)S(1)}, u32[]{:S(2)}, u32[]{:S(2)}) async-start(bf16[3,128,64,2]{1,3,0,2:T(2,128)(2,1)} %copy.148), calls=%async_computation.1 | async-start | bytes 196608 | tf_op jit(solution)/shard_map/all_to_all | solution.py:113
  151.2 59.9 %copy-start.16 = (f32[128,16]{0,1:T(8,128)}, f32[128,16]{0,1:T(8,128)S(1)}, u32[]{:S(2)}) copy-start(f32[128,16]{0,1:T(8,128)S(1)} %copy.150) | copy-start | bytes 24580
  211.1 0.7 copy-start.18
  211.1 0.7 copy-start.20
  (12 other events, 8.0 us)
where the time goes:
time: 242 us; the launch traced here: 238 us
  blocking collectives  144 us (60%)
  local copies, waits for them, and re-layouts  39.1 us (16%)
  starting transfers between devices  22.7 us (9%)
  waiting for transfers between devices  14.5 us (6%)
  other arithmetic  11.6 us (5%)
  between operations  3.21 us (1%)
  matrix products  2.62 us (1%)
    all_gather x1, blocking collectives, on_device(): lax.all_gather(res_sum, 'ctx', axis=1, tiled=True)  63.7 us
    all_gather x1, blocking collectives, on_device(): lax.all_gather(rate_sum, 'ctx', axis=1, tiled=True)  59.6 us
    psum x1, blocking collectives, on_device(): filter_norm = jnp.sqrt(lax.psum(squares, 'chan'))  20.9 us
    all_to_all x1, starting transfers between devices, on_device(): lax.all_to_all(stacked, 'ctx', split_axis=2, concat_axis=2, tiled=True)  18.3 us
    unnamed x90, local copies, waits for them, and re-layouts  16 us
    all_to_all x1, waiting for transfers between devices, on_device(): lax.all_to_all(stacked, 'ctx', split_axis=2, concat_axis=2, tiled=True)  14.5 us
    pad x24, local copies, waits for them, and re-layouts, block_prefix(): inclusive = lax.associative_scan(combine, pieces, axis=1, reverse=reverse)  13.1 us
    slice x23, local copies, waits for them, and re-layouts, block_prefix(): inclusive = lax.associative_scan(combine, pieces, axis=1, reverse=reverse)  4.84 us
  transfers between devices with their start and end apart: 2, of which 1 were waited for; matrix products, arithmetic and copies ran while one was open for 2% of the time, Pallas kernels for 0%

commit v1 on v0

v1 whole, which is shorter than its diff:
```python
import jax
import jax.numpy as jnp
from jax import lax
from jax.experimental import pallas as pl
from jax.experimental.pallas import tpu as pltpu
from jax.sharding import Mesh, PartitionSpec as P

ROWS = 128
LANES = 128
MODES = 16
GROUP = 4
NEAR = 2
RING = 8
BLOCKS = NEAR * GROUP
SHARE = MODES // GROUP
CHANS = 8
TOTAL = ROWS * BLOCKS * RING
F32 = jnp.float32
VM = pl.BlockSpec(memory_space=pltpu.VMEM)


def group_index():
    return lax.axis_index("yl") * 2 + lax.axis_index("core")


def summary_kernel(q_ref, k_ref, v_ref, g_ref, rate_ref, res_ref, out_ref, own_ref, x_s, g_s):
    x_s[...] = k_ref[...].astype(F32) * v_ref[...].astype(F32)
    g_s[...] = g_ref[...].astype(F32) * q_ref[...].astype(F32)
    f = jnp.exp(-rate_ref[...])
    zero = jnp.zeros((MODES, LANES), F32)
    state, moment, adj, sec, res_sum, rate_sum = zero, zero, zero, zero, zero, zero
    for i in range(ROWS):
        j = ROWS - 1 - i
        moment = f * (moment + state)
        state = f * state + x_s[i : i + 1, :]
        sec = f * (sec + adj)
        adj = f * adj + g_s[j : j + 1, :]
        x_j = x_s[j : j + 1, :]
        res_sum = res_sum + x_j * adj
        rate_sum = rate_sum + x_j * sec
    for near in range(NEAR):
        for peer in range(GROUP):
            for at, part in enumerate((state, moment, adj, sec, res_sum, rate_sum)):
                rows = slice(SHARE * at, SHARE * (at + 1))
                out_ref[near * GROUP + peer, rows, :] = part[SHARE * peer : SHARE * (peer + 1)]
    me = group_index()
    for at, ref in enumerate((rate_ref, res_ref)):
        mine = jnp.zeros((SHARE, LANES), F32)
        for peer in range(GROUP):
            mine = jnp.where(me == peer, ref[SHARE * peer : SHARE * (peer + 1), :], mine)
        own_ref[SHARE * at : SHARE * (at + 1), :] = mine


def parts_of(ref, at):
    return tuple(ref[at, SHARE * k : SHARE * (k + 1), :] for k in range(6))


def near_kernel(in_ref, own_ref, out_ref):
    rate = own_ref[0:SHARE, :]
    f = jnp.exp(-rate)
    span = jnp.exp(-rate * ROWS)
    blocks = [parts_of(in_ref, d) for d in range(BLOCKS)]
    state, moment, _, _, res_sum, rate_sum = blocks[0]
    for d in range(1, BLOCKS):
        moment = span * (moment + ROWS * state) + blocks[d][1]
        state = span * state + blocks[d][0]
        res_sum = res_sum + blocks[d][4]
        rate_sum = rate_sum + blocks[d][5]
    adj, sec = blocks[-1][2], blocks[-1][3]
    for d in range(BLOCKS - 2, -1, -1):
        held = f * blocks[d][0]
        held_moment = f * (blocks[d][1] + blocks[d][0])
        res_sum = res_sum + held * adj
        rate_sum = rate_sum + held_moment * adj + held * sec
        sec = span * (sec + ROWS * adj) + blocks[d][3]
        adj = span * adj + blocks[d][2]
    for at, part in enumerate((state, moment, adj, sec, res_sum, rate_sum)):
        for z in range(RING):
            out_ref[z, SHARE * at : SHARE * (at + 1), :] = part


def ring_kernel(ring_ref, in_ref, own_ref, out_ref):
    ring_me, near_me = lax.axis_index("far"), lax.axis_index("near")
    rate = own_ref[0:SHARE, :]
    res = own_ref[SHARE : 2 * SHARE, :]
    f = jnp.exp(-rate)
    span = jnp.exp(-rate * ROWS)
    reach = ROWS * BLOCKS
    long = jnp.exp(-rate * reach)
    zero = jnp.zeros((SHARE, LANES), F32)
    enter = zero
    for z in range(RING - 1):
        enter = jnp.where(z < ring_me, long * enter + ring_ref[z, 0:SHARE, :], enter)
    adj, sec, leave, res_sum, rate_sum = zero, zero, zero, zero, zero
    for z in range(RING - 1, -1, -1):
        state, moment, adj_z, sec_z, res_z, rate_z = parts_of(ring_ref, z)
        leave = jnp.where(z == ring_me, adj, leave)
        held = f * state
        held_moment = f * (moment + state)
        res_sum = res_sum + res_z + held * adj
        rate_sum = rate_sum + rate_z + held_moment * adj + held * sec
        sec = long * (sec + reach * adj) + sec_z
        adj = long * adj + adj_z
    grad_res = res_sum * (1.0 / TOTAL)
    grad_rate = -rate * res * rate_sum * (1.0 / TOTAL)
    enters, leaves = [enter], [leave]
    for d in range(BLOCKS - 1):
        enters.append(span * enters[-1] + in_ref[d, 0:SHARE, :])
        leaves.append(span * leaves[-1] + in_ref[BLOCKS - 1 - d, 2 * SHARE : 3 * SHARE, :])
    leaves = leaves[::-1]
    for d in range(GROUP):
        mine = [jnp.where(near_me == 0, many[d], many[GROUP + d]) for many in (enters, leaves)]
        for chan in range(CHANS):
            for at, part in enumerate((*mine, grad_res, grad_rate)):
                out_ref[chan * GROUP + d, SHARE * at : SHARE * (at + 1), :] = part


def final_kernel(
    back_ref, q_ref, k_ref, v_ref, g_ref, rate_ref, res_ref,
    gq_ref, gk_ref, gv_ref, gres_ref, grate_ref, norm_ref, x_s, g_s,
):
    first = (lax.axis_index("x") * 2 + lax.axis_index("yh")) * GROUP
    x_s[...] = k_ref[...].astype(F32) * v_ref[...].astype(F32)
    g_s[...] = g_ref[...].astype(F32) * q_ref[...].astype(F32)
    f = jnp.exp(-rate_ref[...])
    res = res_ref[...]

    def gathered(at):
        return jnp.concatenate([back_ref[first + d, SHARE * at : SHARE * (at + 1), :] for d in range(GROUP)], axis=0)

    squares = jnp.zeros((2 * SHARE, LANES), F32)
    for peer in range(CHANS * GROUP):
        part = back_ref[peer, 2 * SHARE : 4 * SHARE, :]
        squares = squares + part * part
    norm_ref[...] = jnp.sqrt(jnp.sum(squares, keepdims=True))
    gres_ref[...] = gathered(2)
    grate_ref[...] = gathered(3)
    state = gathered(0)
    adj = gathered(1)
    step = 16
    for base in range(0, ROWS, step):
        conv, grad = [], []
        for i in range(base, base + step):
            j = ROWS - 1 - i
            state = f * state + x_s[i : i + 1, :]
            adj = f * adj + g_s[j : j + 1, :]
            conv.append(jnp.sum(res * state, axis=0, keepdims=True))
            grad.append(jnp.sum(res * adj, axis=0, keepdims=True))
        conv = jnp.concatenate(conv, axis=0)
        grad = jnp.concatenate(grad[::-1], axis=0)
        rows = slice(base, base + step)
        gq_ref[rows, :] = (g_ref[rows, :].astype(F32) * conv).astype(jnp.bfloat16)
        rows = slice(ROWS - base - step, ROWS - base)
        gk_ref[rows, :] = (v_ref[rows, :].astype(F32) * grad).astype(jnp.bfloat16)
        gv_ref[rows, :] = (k_ref[rows, :].astype(F32) * grad).astype(jnp.bfloat16)


def call(kernel, shapes, scratch=(), vmem_in=True, vmem_out=True):
    run = pl.pallas_call(
        kernel,
        out_shape=[(pltpu.VMEM if vmem_out else jax.ShapeDtypeStruct)(s, t) for s, t in shapes],
        out_specs=[VM] * len(shapes),
        scratch_shapes=list(scratch),
    )
    if not vmem_in:
        return run
    return lambda *args: run(*[pltpu.with_memory_space_constraint(a, pltpu.VMEM) for a in args])


def on_device(query_in, key_in, value_in, grad_out, residue, decay_rate):
    block = pltpu.VMEM((ROWS, LANES), F32)
    summary, own = call(
        summary_kernel, [((BLOCKS, 6 * SHARE, LANES), F32), ((2 * SHARE, LANES), F32)], [block, block], vmem_in=False
    )(query_in, key_in, value_in, grad_out, decay_rate, residue)
    near = lax.all_to_all(summary, ("near", "yl", "core"), split_axis=0, concat_axis=0, tiled=True)
    (composite,) = call(near_kernel, [((RING, 6 * SHARE, LANES), F32)])(near, own)
    ring = lax.all_to_all(composite, "far", split_axis=0, concat_axis=0, tiled=True)
    (message,) = call(ring_kernel, [((CHANS * GROUP, 4 * SHARE, LANES), F32)])(ring, near, own)
    back = lax.all_to_all(message, ("x", "yh", "yl", "core"), split_axis=0, concat_axis=0, tiled=True)
    bf = jnp.bfloat16
    gq, gk, gv, gres, grate, norm = call(
        final_kernel,
        [((ROWS, LANES), bf)] * 3 + [((MODES, LANES), F32)] * 2 + [((1, 1), F32)],
        [block, block],
        vmem_out=False,
    )(back, query_in, key_in, value_in, grad_out, decay_rate, residue)
    return gq, gk, gv, gres, grate, norm.reshape(())


def solution(mesh):
    fine = Mesh(mesh.devices.reshape(RING, NEAR, 2, 2, 4, 2), ("far", "near", "yl", "core", "x", "yh"))
    ctx, chan = ("far", "near", "yl", "core"), ("x", "yh")
    return jax.shard_map(
        on_device,
        mesh=fine,
        in_specs=(P(ctx, chan),) * 4 + (P(None, chan),) * 2,
        out_specs=(P(ctx, chan),) * 3 + (P(None, chan),) * 2 + (P(),),
        check_vma=False,
    )
```

time: 242 us -> 58.5 us (0.24); the launches traced: 238 us -> 58.2 us
  blocking collectives: 144 us -> 54.9 us
  local copies, waits for them, and re-layouts: 39.1 us -> 0.04 us
  starting transfers between devices: 22.7 us -> 0 us
  waiting for transfers between devices: 14.5 us -> 0 us
  other arithmetic: 11.6 us -> 0 us
  matrix products: 2.62 us -> 0 us
  Pallas kernels: 0 us -> 2.55 us
  between operations: 3.21 us -> 0.72 us
    all_gather x2 -> x0, blocking collectives: 123 us -> none  [the longest x1 63.7 us: on_device(): lax.all_gather(res_sum, 'ctx', axis=1, tiled=True)]
    all_to_all x0 -> x3, blocking collectives: none -> 54.9 us  [the longest x1 22.7 us: on_device(): lax.all_to_all(composite, 'far', split_axis=0, concat_axis=0, tiled=True)]
    all_to_all x2 -> x0, starting transfers between devices: 22.7 us -> none  [the longest x1 18.3 us: on_device(): lax.all_to_all(stacked, 'ctx', split_axis=2, concat_axis=2, tiled=True)]
    psum x1 -> x0, blocking collectives: 20.9 us -> none  [on_device(): filter_norm = jnp.sqrt(lax.psum(squares, 'chan'))]
    unnamed x90 -> x12, local copies, waits for them, and re-layouts: 16 us -> 0.04 us
    all_to_all x2 -> x0, waiting for transfers between devices: 14.5 us -> none  [the longest x1 14.5 us: on_device(): lax.all_to_all(stacked, 'ctx', split_axis=2, concat_axis=2, tiled=True)]
    pad x24 -> x0, local copies, waits for them, and re-layouts: 13.1 us -> none  [block_prefix(): inclusive = lax.associative_scan(combine, pieces, axis=1, reverse=reverse)]
    add x39 -> x0, other arithmetic: 6.61 us -> none  [the longest x18 3.25 us: block_prefix(): inclusive = lax.associative_scan(combine, pieces, axis=1, reverse=reverse)]
  transfers between devices with their start and end apart: 2 -> 0, of which waited for: 1 -> 0; matrix products, arithmetic and copies ran while one was open for 2% -> 0% of each run, Pallas kernels for 0% -> 0%
where the time goes in v1:
time: 58.5 us; the launch traced here: 58.2 us
  blocking collectives  54.9 us (94%)
  Pallas kernels  2.55 us (4%)
  between operations  0.72 us (1%)
    all_to_all x1, blocking collectives, on_device(): lax.all_to_all(composite, 'far', split_axis=0, concat_axis=0, tiled=True)  22.7 us
    all_to_all x1, blocking collectives, on_device(): lax.all_to_all(message, ('x', 'yh', 'yl', 'core'), split_axis=0, concat_a...  18.8 us
    all_to_all x1, blocking collectives, on_device(): lax.all_to_all(summary, ('near', 'yl', 'core'), split_axis=0, concat_axis...  13.4 us
    pallas_call x3, Pallas kernels, call(): run(*[pltpu.with_memory_space_constraint(a, pltpu.VMEM) for a in args])  1.3 us
    pallas_call x1, Pallas kernels, on_device(): call(summary_kernel, [((BLOCKS, 6 * SHARE, LANES), F32), ((2 * SHARE, LAN...  1.25 us

profile of v1, /device:TPU:1, one launch (start us, length us, event | category | flops | bytes accessed | tf_op | source)
XLA Modules:
  0.0 58.2 jit_solution(16640209736896053652)
XLA Ops:
  0.6 1.2 %shard_map.109 = (f32[8,24,128]{2,1,0:T(8,128)S(1)}, f32[8,128]{1,0:T(8,128)S(1)}) custom-call(bf16[128,128]{1,0:T(8,128)(2,1)} %q_ref.3, bf16[128,128]{1,0:T(8,128)(2,1)} %k_ref.3, bf16[128,128]{1,0:T(8,128)(2,1)} %v_ref.3, bf16[128,128]{1,0:T(8,128)(2,1)} %g_ref.3, f32[16,128]{1,0:T(8,128)} %rate_ref.3, f32[16,128]{1,0:T(8,128)} %res_ref.3), custom_call_target="tpu_custom_call" | custom-call | tf_op jit(solution)/shard_map/pallas_call | solution.py:172
  1.9 13.4 %all_to_all.15.in_ref = f32[8,24,128]{2,1,0:T(8,128)S(1)} all-to-all(f32[8,24,128]{2,1,0:T(8,128)S(1)} %get-tuple-element.14), channel_id=1, replica_groups=mesh['far'=8,'near'=2,'yl'=2,'core'=2,'x'=4,'yh'=2] {'near','yl','core'}, dimensions={0} | all-to-all | bytes 196608 | tf_op jit(solution)/shard_map/all_to_all | solution.py:175
  15.3 22.7 %all_to_all.16.ring_ref = f32[8,24,128]{2,1,0:T(8,128)S(1)} all-to-all(f32[8,24,128]{2,1,0:T(8,128)S(1)} %shard_map.110), channel_id=1, replica_groups=mesh['far'=8,'near'=2,'yl'=2,'core'=2,'x'=4,'yh'=2] {'far'}, dimensions={0} | all-to-all | bytes 196608 | tf_op jit(solution)/shard_map/all_to_all | solution.py:177
  38.0 0.1 shard_map.111
  38.1 0.0 copy-start
  38.1 0.0 copy-start.1
  38.1 0.0 copy-start.2
  38.1 0.0 copy-start.3
  38.1 0.0 copy-start.4
  38.2 0.0 copy-start.5
  38.2 18.8 %all_to_all.17.back_ref = f32[32,16,128]{2,1,0:T(8,128)S(1)} all-to-all(f32[32,16,128]{2,1,0:T(8,128)S(1)} %shard_map.111), channel_id=1, replica_groups=mesh['far'=8,'near'=2,'yl'=2,'core'=2,'x'=4,'yh'=2] {'x','yh','yl','core'}, dimensions={0} | all-to-all | bytes 524288 | tf_op jit(solution)/shard_map/all_to_all | solution.py:179
  57.0 0.0 copy-done
  57.0 0.0 copy-done.1
  57.0 0.0 copy-done.2
  57.0 0.0 copy-done.3
  57.0 0.0 copy-done.4
  57.0 0.0 copy-done.5
  57.0 1.2 %shard_map.112 = (bf16[128,128]{1,0:T(8,128)(2,1)}, bf16[128,128]{1,0:T(8,128)(2,1)}, bf16[128,128]{1,0:T(8,128)(2,1)}, f32[16,128]{1,0:T(8,128)}, f32[16,128]{1,0:T(8,128)}, /*index=5*/f32[1,1]{1,0:T(1,128)}) custom-call(f32[32,16,128]{2,1,0:T(8,128)S(1)} %all_to_all.17.back_ref, bf16[128,128]{1,0:T(8,128)(2,1)S(1)} %copy-done, ...), custom_call_target="tpu_custom_call" | custom-call | tf_op jit(solution)/shard_map/pallas_call | solution.py:167
  (1 shorter events, 0.0 us)
Async XLA Ops:
  38.1 18.9 %copy-start = (bf16[128,128]{1,0:T(8,128)(2,1)S(1)}, bf16[128,128]{1,0:T(8,128)(2,1)}, u32[]{:S(2)}) copy-start(bf16[128,128]{1,0:T(8,128)(2,1)} %q_ref.3) | copy-start | bytes 98308
  38.1 18.9 %copy-start.1 = (bf16[128,128]{1,0:T(8,128)(2,1)S(1)}, bf16[128,128]{1,0:T(8,128)(2,1)}, u32[]{:S(2)}) copy-start(bf16[128,128]{1,0:T(8,128)(2,1)} %k_ref.3) | copy-start | bytes 98308
  38.1 18.9 %copy-start.2 = (bf16[128,128]{1,0:T(8,128)(2,1)S(1)}, bf16[128,128]{1,0:T(8,128)(2,1)}, u32[]{:S(2)}) copy-start(bf16[128,128]{1,0:T(8,128)(2,1)} %v_ref.3) | copy-start | bytes 98308
  38.1 18.9 %copy-start.3 = (bf16[128,128]{1,0:T(8,128)(2,1)S(1)}, bf16[128,128]{1,0:T(8,128)(2,1)}, u32[]{:S(2)}) copy-start(bf16[128,128]{1,0:T(8,128)(2,1)} %g_ref.3) | copy-start | bytes 98308
  38.1 18.9 %copy-start.4 = (f32[16,128]{1,0:T(8,128)S(1)}, f32[16,128]{1,0:T(8,128)}, u32[]{:S(2)}) copy-start(f32[16,128]{1,0:T(8,128)} %rate_ref.3) | copy-start | bytes 24580
  38.2 18.9 %copy-start.5 = (f32[16,128]{1,0:T(8,128)S(1)}, f32[16,128]{1,0:T(8,128)}, u32[]{:S(2)}) copy-start(f32[16,128]{1,0:T(8,128)} %res_ref.3) | copy-start | bytes 24580

commit v2 on v1

--- a/solution.py
+++ b/solution.py
@@ -14,6 +14,9 @@
 BLOCKS = NEAR * GROUP
 SHARE = MODES // GROUP
 CHANS = 8
+NEAR_FIRST = 4
+RING_FIRST = 4
+PLANE_FIRST = 20
 TOTAL = ROWS * BLOCKS * RING
 F32 = jnp.float32
 VM = pl.BlockSpec(memory_space=pltpu.VMEM)
@@ -42,7 +45,7 @@
         for peer in range(GROUP):
             for at, part in enumerate((state, moment, adj, sec, res_sum, rate_sum)):
                 rows = slice(SHARE * at, SHARE * (at + 1))
-                out_ref[near * GROUP + peer, rows, :] = part[SHARE * peer : SHARE * (peer + 1)]
+                out_ref[(near * GROUP + peer) ^ NEAR_FIRST, rows, :] = part[SHARE * peer : SHARE * (peer + 1)]
     me = group_index()
     for at, ref in enumerate((rate_ref, res_ref)):
         mine = jnp.zeros((SHARE, LANES), F32)
@@ -59,7 +62,7 @@
     rate = own_ref[0:SHARE, :]
     f = jnp.exp(-rate)
     span = jnp.exp(-rate * ROWS)
-    blocks = [parts_of(in_ref, d) for d in range(BLOCKS)]
+    blocks = [parts_of(in_ref, d ^ NEAR_FIRST) for d in range(BLOCKS)]
     state, moment, _, _, res_sum, rate_sum = blocks[0]
     for d in range(1, BLOCKS):
         moment = span * (moment + ROWS * state) + blocks[d][1]
@@ -90,10 +93,10 @@
     zero = jnp.zeros((SHARE, LANES), F32)
     enter = zero
     for z in range(RING - 1):
-        enter = jnp.where(z < ring_me, long * enter + ring_ref[z, 0:SHARE, :], enter)
+        enter = jnp.where(z < ring_me, long * enter + ring_ref[z ^ RING_FIRST, 0:SHARE, :], enter)
     adj, sec, leave, res_sum, rate_sum = zero, zero, zero, zero, zero
     for z in range(RING - 1, -1, -1):
-        state, moment, adj_z, sec_z, res_z, rate_z = parts_of(ring_ref, z)
+        state, moment, adj_z, sec_z, res_z, rate_z = parts_of(ring_ref, z ^ RING_FIRST)
         leave = jnp.where(z == ring_me, adj, leave)
         held = f * state
         held_moment = f * (moment + state)
@@ -105,28 +108,28 @@
     grad_rate = -rate * res * rate_sum * (1.0 / TOTAL)
     enters, leaves = [enter], [leave]
     for d in range(BLOCKS - 1):
-        enters.append(span * enters[-1] + in_ref[d, 0:SHARE, :])
-        leaves.append(span * leaves[-1] + in_ref[BLOCKS - 1 - d, 2 * SHARE : 3 * SHARE, :])
+        enters.append(span * enters[-1] + in_ref[d ^ NEAR_FIRST, 0:SHARE, :])
+        leaves.append(span * leaves[-1] + in_ref[(BLOCKS - 1 - d) ^ NEAR_FIRST, 2 * SHARE : 3 * SHARE, :])
     leaves = leaves[::-1]
     for d in range(GROUP):
         mine = [jnp.where(near_me == 0, many[d], many[GROUP + d]) for many in (enters, leaves)]
         for chan in range(CHANS):
             for at, part in enumerate((*mine, grad_res, grad_rate)):
-                out_ref[chan * GROUP + d, SHARE * at : SHARE * (at + 1), :] = part
+                out_ref[(chan * GROUP + d) ^ PLANE_FIRST, SHARE * at : SHARE * (at + 1), :] = part
 
 
 def final_kernel(
     back_ref, q_ref, k_ref, v_ref, g_ref, rate_ref, res_ref,
     gq_ref, gk_ref, gv_ref, gres_ref, grate_ref, norm_ref, x_s, g_s,
 ):
-    first = (lax.axis_index("x") * 2 + lax.axis_index("yh")) * GROUP
+    first = ((lax.axis_index("x") * 2 + lax.axis_index("yh")) ^ (PLANE_FIRST // GROUP)) * GROUP
     x_s[...] = k_ref[...].astype(F32) * v_ref[...].astype(F32)
     g_s[...] = g_ref[...].astype(F32) * q_ref[...].astype(F32)
     f = jnp.exp(-rate_ref[...])
     res = res_ref[...]
 
     def gathered(at):
-        return jnp.concatenate([back_ref[first + d, SHARE * at : SHARE * (at + 1), :] for d in range(GROUP)], axis=0)
+        return jnp.concatenate([back_ref[first + (d ^ (PLANE_FIRST % GROUP)), SHARE * at : SHARE * (at + 1), :] for d in range(GROUP)], axis=0)
 
     squares = jnp.zeros((2 * SHARE, LANES), F32)
     for peer in range(CHANS * GROUP):
@@ -167,16 +170,21 @@
     return lambda *args: run(*[pltpu.with_memory_space_constraint(a, pltpu.VMEM) for a in args])
 
 
+def exchange(blocks, axes, first):
+    order = [p ^ first for p in range(blocks.shape[0])]
+    return lax.all_to_all(blocks, axes, split_axis=0, concat_axis=0, axis_index_groups=[order], tiled=True)
+
+
 def on_device(query_in, key_in, value_in, grad_out, residue, decay_rate):
     block = pltpu.VMEM((ROWS, LANES), F32)
     summary, own = call(
         summary_kernel, [((BLOCKS, 6 * SHARE, LANES), F32), ((2 * SHARE, LANES), F32)], [block, block], vmem_in=False
     )(query_in, key_in, value_in, grad_out, decay_rate, residue)
-    near = lax.all_to_all(summary, ("near", "yl", "core"), split_axis=0, concat_axis=0, tiled=True)
+    near = exchange(summary, ("near", "yl", "core"), NEAR_FIRST)
     (composite,) = call(near_kernel, [((RING, 6 * SHARE, LANES), F32)])(near, own)
-    ring = lax.all_to_all(composite, "far", split_axis=0, concat_axis=0, tiled=True)
+    ring = exchange(composite, "far", RING_FIRST)
     (message,) = call(ring_kernel, [((CHANS * GROUP, 4 * SHARE, LANES), F32)])(ring, near, own)
-    back = lax.all_to_all(message, ("x", "yh", "yl", "core"), split_axis=0, concat_axis=0, tiled=True)
+    back = exchange(message, ("x", "yh", "yl", "core"), PLANE_FIRST)
     bf = jnp.bfloat16
     gq, gk, gv, gres, grate, norm = call(
         final_kernel,

time: 58.5 us -> 47.8 us (0.82)
  blocking collectives: 54.9 us -> 44.1 us
    all_to_all x3, blocking collectives: 54.9 us -> 44.1 us  [exchange(): lax.all_to_all(blocks, axes, split_axis=0, concat_axis=0, axis_index_grou...]
where the time goes in v2:
time: 47.8 us; the launch traced here: 47.4 us
  blocking collectives  44.1 us (92%)
  Pallas kernels  2.55 us (5%)
  between operations  0.72 us (2%)
    all_to_all x3, blocking collectives, exchange(): lax.all_to_all(blocks, axes, split_axis=0, concat_axis=0, axis_index_grou...  44.1 us
    pallas_call x3, Pallas kernels, call(): run(*[pltpu.with_memory_space_constraint(a, pltpu.VMEM) for a in args])  1.3 us
    pallas_call x1, Pallas kernels, on_device(): call(summary_kernel, [((BLOCKS, 6 * SHARE, LANES), F32), ((2 * SHARE, LAN...  1.25 us

profile of v2, /device:TPU:1, one launch (start us, length us, event | category | flops | bytes accessed | tf_op | source)
XLA Modules:
  0.0 47.4 jit_solution(11812598525313888081)
XLA Ops:
  0.6 1.2 %shard_map.109 = (f32[8,24,128]{2,1,0:T(8,128)S(1)}, f32[8,128]{1,0:T(8,128)S(1)}) custom-call(bf16[128,128]{1,0:T(8,128)(2,1)} %q_ref.3, bf16[128,128]{1,0:T(8,128)(2,1)} %k_ref.3, bf16[128,128]{1,0:T(8,128)(2,1)} %v_ref.3, bf16[128,128]{1,0:T(8,128)(2,1)} %g_ref.3, f32[16,128]{1,0:T(8,128)} %rate_ref.3, f32[16,128]{1,0:T(8,128)} %res_ref.3), custom_call_target="tpu_custom_call" | custom-call | tf_op jit(solution)/shard_map/pallas_call | solution.py:180
  1.9 13.0 %all_to_all.15.in_ref = f32[8,24,128]{2,1,0:T(8,128)S(1)} all-to-all(f32[8,24,128]{2,1,0:T(8,128)S(1)} %get-tuple-element.14), channel_id=1, replica_groups={{32,40,48,56,0,8,16,24},{33,41,49,57,1,9,17,25},{34,42,50,58,2,10,18,26..., dimensions={0} | all-to-all | bytes 196608 | tf_op jit(solution)/shard_map/all_to_all | solution.py:175
  15.0 16.7 %all_to_all.16.ring_ref = f32[8,24,128]{2,1,0:T(8,128)S(1)} all-to-all(f32[8,24,128]{2,1,0:T(8,128)S(1)} %shard_map.110), channel_id=1, replica_groups={{256,320,384,448,0,64,128,192},{257,321,385,449,1,65,129,193},{258,322,..., dimensions={0} | all-to-all | bytes 196608 | tf_op jit(solution)/shard_map/all_to_all | solution.py:175
  31.7 0.1 shard_map.111
  31.8 0.0 copy-start
  31.8 0.0 copy-start.1
  31.8 0.0 copy-start.2
  31.8 0.0 copy-start.3
  31.8 0.0 copy-start.4
  31.8 0.0 copy-start.5
  31.9 14.3 %all_to_all.17.back_ref = f32[32,16,128]{2,1,0:T(8,128)S(1)} all-to-all(f32[32,16,128]{2,1,0:T(8,128)S(1)} %shard_map.111), channel_id=1, replica_groups={{5,13,21,29,4,12,20,28,7,15,23,31,6,14,22,30,1,9,17,25,0,8,16,24,3,11,1..., dimensions={0} | all-to-all | bytes 524288 | tf_op jit(solution)/shard_map/all_to_all | solution.py:175
  46.2 0.0 copy-done
  46.2 0.0 copy-done.1
  46.2 0.0 copy-done.2
  46.2 0.0 copy-done.3
  46.2 0.0 copy-done.4
  46.2 0.0 copy-done.5
  46.2 1.2 %shard_map.112 = (bf16[128,128]{1,0:T(8,128)(2,1)}, bf16[128,128]{1,0:T(8,128)(2,1)}, bf16[128,128]{1,0:T(8,128)(2,1)}, f32[16,128]{1,0:T(8,128)}, f32[16,128]{1,0:T(8,128)}, /*index=5*/f32[1,1]{1,0:T(1,128)}) custom-call(f32[32,16,128]{2,1,0:T(8,128)S(1)} %all_to_all.17.back_ref, bf16[128,128]{1,0:T(8,128)(2,1)S(1)} %copy-done, ...), custom_call_target="tpu_custom_call" | custom-call | tf_op jit(solution)/shard_map/pallas_call | solution.py:170
  (1 shorter events, 0.0 us)
Async XLA Ops:
  31.8 14.4 %copy-start = (bf16[128,128]{1,0:T(8,128)(2,1)S(1)}, bf16[128,128]{1,0:T(8,128)(2,1)}, u32[]{:S(2)}) copy-start(bf16[128,128]{1,0:T(8,128)(2,1)} %q_ref.3) | copy-start | bytes 98308
  31.8 14.4 %copy-start.1 = (bf16[128,128]{1,0:T(8,128)(2,1)S(1)}, bf16[128,128]{1,0:T(8,128)(2,1)}, u32[]{:S(2)}) copy-start(bf16[128,128]{1,0:T(8,128)(2,1)} %k_ref.3) | copy-start | bytes 98308
  31.8 14.4 %copy-start.2 = (bf16[128,128]{1,0:T(8,128)(2,1)S(1)}, bf16[128,128]{1,0:T(8,128)(2,1)}, u32[]{:S(2)}) copy-start(bf16[128,128]{1,0:T(8,128)(2,1)} %v_ref.3) | copy-start | bytes 98308
  31.8 14.4 %copy-start.3 = (bf16[128,128]{1,0:T(8,128)(2,1)S(1)}, bf16[128,128]{1,0:T(8,128)(2,1)}, u32[]{:S(2)}) copy-start(bf16[128,128]{1,0:T(8,128)(2,1)} %g_ref.3) | copy-start | bytes 98308
  31.8 14.4 %copy-start.4 = (f32[16,128]{1,0:T(8,128)S(1)}, f32[16,128]{1,0:T(8,128)}, u32[]{:S(2)}) copy-start(f32[16,128]{1,0:T(8,128)} %rate_ref.3) | copy-start | bytes 24580
  31.8 14.4 %copy-start.5 = (f32[16,128]{1,0:T(8,128)S(1)}, f32[16,128]{1,0:T(8,128)}, u32[]{:S(2)}) copy-start(f32[16,128]{1,0:T(8,128)} %res_ref.3) | copy-start | bytes 24580

commit v3 on v2

--- a/solution.py
+++ b/solution.py
@@ -15,10 +15,14 @@
 SHARE = MODES // GROUP
 CHANS = 8
 NEAR_FIRST = 4
-RING_FIRST = 4
+RING_ORDER = (4, 0, 5, 1, 6, 2, 7, 3)
 PLANE_FIRST = 20
 TOTAL = ROWS * BLOCKS * RING
 F32 = jnp.float32
+TINY = 1e-37
+RING_CODES = ((256.0, 1), (8.0, 1), (256.0, 1), (8.0, 1), (256.0, 2), (64.0, 2))
+CARRY_CODE = (64.0, 1)
+GRAD_CODE = (1024.0, 2)
 VM = pl.BlockSpec(memory_space=pltpu.VMEM)
 
 
@@ -26,9 +30,15 @@
     return lax.axis_index("yl") * 2 + lax.axis_index("core")
 
 
-def summary_kernel(q_ref, k_ref, v_ref, g_ref, rate_ref, res_ref, out_ref, own_ref, x_s, g_s):
+def summary_kernel(
+    q_ref, k_ref, v_ref, g_ref, rate_ref, res_ref,
+    out_ref, own_ref, x_s, g_s, k_keep, v_keep, g_keep, rate_keep, res_keep,
+):
     x_s[...] = k_ref[...].astype(F32) * v_ref[...].astype(F32)
     g_s[...] = g_ref[...].astype(F32) * q_ref[...].astype(F32)
+    kept = ((k_keep, k_ref), (v_keep, v_ref), (g_keep, g_ref), (rate_keep, rate_ref), (res_keep, res_ref))
+    for keep, ref in kept:
+        keep[...] = ref[...]
     f = jnp.exp(-rate_ref[...])
     zero = jnp.zeros((MODES, LANES), F32)
     state, moment, adj, sec, res_sum, rate_sum = zero, zero, zero, zero, zero, zero
@@ -54,8 +64,26 @@
         own_ref[SHARE * at : SHARE * (at + 1), :] = mine
 
 
-def parts_of(ref, at):
-    return tuple(ref[at, SHARE * k : SHARE * (k + 1), :] for k in range(6))
+def rooted(v):
+    return v * lax.rsqrt(jnp.abs(v) + TINY)
+
+
+def coded(v, gain, roots):
+    for _ in range(roots):
+        v = rooted(v)
+    return v * gain
+
+
+def decoded(y, gain, roots):
+    y = y * (1.0 / gain)
+    for _ in range(roots):
+        y = y * jnp.abs(y)
+    return y
+
+
+def parts_of(ref, at, codes=None):
+    parts = tuple(ref[at, SHARE * k : SHARE * (k + 1), :] for k in range(6))
+    return parts if codes is None else tuple(decoded(p, *c) for p, c in zip(parts, codes))
 
 
 def near_kernel(in_ref, own_ref, out_ref):
@@ -78,6 +106,7 @@
         sec = span * (sec + ROWS * adj) + blocks[d][3]
         adj = span * adj + blocks[d][2]
     for at, part in enumerate((state, moment, adj, sec, res_sum, rate_sum)):
+        part = coded(part, *RING_CODES[at])
         for z in range(RING):
             out_ref[z, SHARE * at : SHARE * (at + 1), :] = part
 
@@ -91,12 +120,13 @@
     reach = ROWS * BLOCKS
     long = jnp.exp(-rate * reach)
     zero = jnp.zeros((SHARE, LANES), F32)
+    composites = [parts_of(ring_ref, RING_ORDER.index(z), RING_CODES) for z in range(RING)]
     enter = zero
     for z in range(RING - 1):
-        enter = jnp.where(z < ring_me, long * enter + ring_ref[z ^ RING_FIRST, 0:SHARE, :], enter)
+        enter = jnp.where(z < ring_me, long * enter + composites[z][0], enter)
     adj, sec, leave, res_sum, rate_sum = zero, zero, zero, zero, zero
     for z in range(RING - 1, -1, -1):
-        state, moment, adj_z, sec_z, res_z, rate_z = parts_of(ring_ref, z ^ RING_FIRST)
+        state, moment, adj_z, sec_z, res_z, rate_z = composites[z]
         leave = jnp.where(z == ring_me, adj, leave)
         held = f * state
         held_moment = f * (moment + state)
@@ -113,33 +143,34 @@
     leaves = leaves[::-1]
     for d in range(GROUP):
         mine = [jnp.where(near_me == 0, many[d], many[GROUP + d]) for many in (enters, leaves)]
+        parts = [coded(p, *CARRY_CODE) for p in mine] + [coded(p, *GRAD_CODE) for p in (grad_res, grad_rate)]
         for chan in range(CHANS):
-            for at, part in enumerate((*mine, grad_res, grad_rate)):
+            for at, part in enumerate(parts):
                 out_ref[(chan * GROUP + d) ^ PLANE_FIRST, SHARE * at : SHARE * (at + 1), :] = part
 
 
 def final_kernel(
-    back_ref, q_ref, k_ref, v_ref, g_ref, rate_ref, res_ref,
-    gq_ref, gk_ref, gv_ref, gres_ref, grate_ref, norm_ref, x_s, g_s,
+    back_ref, x_s, g_s, k_ref, v_ref, g_ref, rate_ref, res_ref,
+    gq_ref, gk_ref, gv_ref, gres_ref, grate_ref, norm_ref,
 ):
     first = ((lax.axis_index("x") * 2 + lax.axis_index("yh")) ^ (PLANE_FIRST // GROUP)) * GROUP
-    x_s[...] = k_ref[...].astype(F32) * v_ref[...].astype(F32)
-    g_s[...] = g_ref[...].astype(F32) * q_ref[...].astype(F32)
     f = jnp.exp(-rate_ref[...])
     res = res_ref[...]
 
-    def gathered(at):
-        return jnp.concatenate([back_ref[first + (d ^ (PLANE_FIRST % GROUP)), SHARE * at : SHARE * (at + 1), :] for d in range(GROUP)], axis=0)
+    def gathered(at, code):
+        rows = slice(SHARE * at, SHARE * (at + 1))
+        parts = [back_ref[first + (d ^ (PLANE_FIRST % GROUP)), rows, :] for d in range(GROUP)]
+        return decoded(jnp.concatenate(parts, axis=0), *code)
 
     squares = jnp.zeros((2 * SHARE, LANES), F32)
     for peer in range(CHANS * GROUP):
-        part = back_ref[peer, 2 * SHARE : 4 * SHARE, :]
+        part = decoded(back_ref[peer, 2 * SHARE : 4 * SHARE, :], *GRAD_CODE)
         squares = squares + part * part
     norm_ref[...] = jnp.sqrt(jnp.sum(squares, keepdims=True))
-    gres_ref[...] = gathered(2)
-    grate_ref[...] = gathered(3)
-    state = gathered(0)
-    adj = gathered(1)
+    gres_ref[...] = gathered(2, GRAD_CODE)
+    grate_ref[...] = gathered(3, GRAD_CODE)
+    state = gathered(0, CARRY_CODE)
+    adj = gathered(1, CARRY_CODE)
     step = 16
     for base in range(0, ROWS, step):
         conv, grad = [], []
@@ -170,28 +201,28 @@
     return lambda *args: run(*[pltpu.with_memory_space_constraint(a, pltpu.VMEM) for a in args])
 
 
-def exchange(blocks, axes, first):
-    order = [p ^ first for p in range(blocks.shape[0])]
-    return lax.all_to_all(blocks, axes, split_axis=0, concat_axis=0, axis_index_groups=[order], tiled=True)
+def exchange(blocks, axes, order):
+    return lax.all_to_all(blocks, axes, split_axis=0, concat_axis=0, axis_index_groups=[list(order)], tiled=True)
 
 
 def on_device(query_in, key_in, value_in, grad_out, residue, decay_rate):
-    block = pltpu.VMEM((ROWS, LANES), F32)
-    summary, own = call(
-        summary_kernel, [((BLOCKS, 6 * SHARE, LANES), F32), ((2 * SHARE, LANES), F32)], [block, block], vmem_in=False
+    bf = jnp.bfloat16
+    block, table = (ROWS, LANES), (MODES, LANES)
+    summary, own, *kept = call(
+        summary_kernel,
+        [((BLOCKS, 6 * SHARE, LANES), F32), ((2 * SHARE, LANES), F32)]
+        + [(block, F32)] * 2 + [(block, bf)] * 3 + [(table, F32)] * 2,
+        vmem_in=False,
     )(query_in, key_in, value_in, grad_out, decay_rate, residue)
-    near = exchange(summary, ("near", "yl", "core"), NEAR_FIRST)
+    near = exchange(summary, ("near", "yl", "core"), [p ^ NEAR_FIRST for p in range(BLOCKS)])
     (composite,) = call(near_kernel, [((RING, 6 * SHARE, LANES), F32)])(near, own)
-    ring = exchange(composite, "far", RING_FIRST)
+    ring = exchange(composite.astype(jnp.float16), "far", RING_ORDER).astype(F32)
     (message,) = call(ring_kernel, [((CHANS * GROUP, 4 * SHARE, LANES), F32)])(ring, near, own)
-    back = exchange(message, ("x", "yh", "yl", "core"), PLANE_FIRST)
-    bf = jnp.bfloat16
+    order = [p ^ PLANE_FIRST for p in range(CHANS * GROUP)]
+    back = exchange(message.astype(jnp.float16), ("x", "yh", "yl", "core"), order).astype(F32)
     gq, gk, gv, gres, grate, norm = call(
-        final_kernel,
-        [((ROWS, LANES), bf)] * 3 + [((MODES, LANES), F32)] * 2 + [((1, 1), F32)],
-        [block, block],
-        vmem_out=False,
-    )(back, query_in, key_in, value_in, grad_out, decay_rate, residue)
+        final_kernel, [(block, bf)] * 3 + [(table, F32)] * 2 + [((1, 1), F32)], vmem_out=False
+    )(back, *kept)
     return gq, gk, gv, gres, grate, norm.reshape(())
 
 

time: 47.8 us -> 44.4 us (0.929)
  blocking collectives: 44.1 us -> 40.8 us
    all_to_all x3, blocking collectives: 44.1 us -> 40.8 us  [exchange(): lax.all_to_all(blocks, axes, split_axis=0, concat_axis=0, axis_index_grou...]
where the time goes in v3:
time: 44.4 us; the launch traced here: 44.1 us
  blocking collectives  40.8 us (92%)
  Pallas kernels  2.61 us (6%)
  between operations  0.67 us (2%)
    all_to_all x3, blocking collectives, exchange(): lax.all_to_all(blocks, axes, split_axis=0, concat_axis=0, axis_index_grou...  40.8 us
    pallas_call x3, Pallas kernels, call(): run(*[pltpu.with_memory_space_constraint(a, pltpu.VMEM) for a in args])  1.36 us
    pallas_call x1, Pallas kernels, on_device(): call(summary_kernel, [((BLOCKS, 6 * SHARE, LANES), F32), ((2 * SHARE, LAN...  1.25 us

profile of v3, /device:TPU:1, one launch (start us, length us, event | category | flops | bytes accessed | tf_op | source)
XLA Modules:
  0.0 44.1 jit_solution(13627052083823812443)
XLA Ops:
  0.6 1.2 %shard_map.109 = (f32[8,24,128]{2,1,0:T(8,128)S(1)}, f32[8,128]{1,0:T(8,128)S(1)}, f32[128,128]{1,0:T(8,128)S(1)}, f32[128,128]{1,0:T(8,128)S(1)}, bf16[128,128]...) custom-call(bf16[128,128]{1,0:T(8,128)(2,1)} %q_ref.1, ...), custom_call_target="tpu_custom_call" | custom-call | tf_op jit(solution)/shard_map/pallas_call | solution.py:211
  1.9 13.0 %all_to_all.15.in_ref = f32[8,24,128]{2,1,0:T(8,128)S(1)} all-to-all(f32[8,24,128]{2,1,0:T(8,128)S(1)} %get-tuple-element.21), channel_id=1, replica_groups={{32,40,48,56,0,8,16,24},{33,41,49,57,1,9,17,25},{34,42,50,58,2,10,18,26..., dimensions={0} | all-to-all | bytes 196608 | tf_op jit(solution)/shard_map/all_to_all | solution.py:205
  14.9 0.1 shard_map.110
  15.0 15.4 %all_to_all.16 = f16[8,24,128]{2,1,0:T(8,128)(2,1)S(1)} all-to-all(f16[8,24,128]{2,1,0:T(8,128)(2,1)S(1)} %convert_element_type.12), channel_id=1, replica_groups={{256,0,320,64,384,128,448,192},{257,1,321,65,385,129,449,193},{258,2,32..., dimensions={0} | all-to-all | bytes 98304 | tf_op jit(solution)/shard_map/all_to_all | solution.py:205
  30.4 0.1 shard_map.111
  30.5 12.3 %all_to_all.17 = f16[32,16,128]{2,1,0:T(8,128)(2,1)S(1)} all-to-all(f16[32,16,128]{2,1,0:T(8,128)(2,1)S(1)} %convert_element_type.14), channel_id=1, replica_groups={{5,13,21,29,4,12,20,28,7,15,23,31,6,14,22,30,1,9,17,25,0,8,16,24,3,11,1..., dimensions={0} | all-to-all | bytes 262144 | tf_op jit(solution)/shard_map/all_to_all | solution.py:205
  42.9 1.2 %shard_map.112 = (bf16[128,128]{1,0:T(8,128)(2,1)}, bf16[128,128]{1,0:T(8,128)(2,1)}, bf16[128,128]{1,0:T(8,128)(2,1)}, f32[16,128]{1,0:T(8,128)}, f32[16,128]{1,0:T(8,128)}, /*index=5*/f32[1,1]{1,0:T(1,128)}) custom-call(f32[32,16,128]{2,1,0:T(8,128)S(1)} %convert_element_type.15.back_ref, f32[128,128]{1,0:T(8,128)S(1)} %get-tuple-element.23.x_s, ...), custom_call_target="tpu_custom_call" | custom-call | tf_op jit(solution)/shard_map/pallas_call | solution.py:201
  (4 shorter events, 0.1 us)

commit v4 on v3

--- a/solution.py
+++ b/solution.py
@@ -14,9 +14,9 @@
 BLOCKS = NEAR * GROUP
 SHARE = MODES // GROUP
 CHANS = 8
-NEAR_FIRST = 4
+NEAR_FIRST = 5
 RING_ORDER = (4, 0, 5, 1, 6, 2, 7, 3)
-PLANE_FIRST = 20
+PLANE_FIRST = 21
 TOTAL = ROWS * BLOCKS * RING
 F32 = jnp.float32
 TINY = 1e-37

time: 44.4 us -> 43.8 us (0.986)
  blocking collectives: 40.8 us -> 40.1 us
    all_to_all x3, blocking collectives: 40.8 us -> 40.1 us  [exchange(): lax.all_to_all(blocks, axes, split_axis=0, concat_axis=0, axis_index_grou...]
where the time goes in v4:
time: 43.8 us; the launch traced here: 43.5 us
  blocking collectives  40.1 us (92%)
  Pallas kernels  2.61 us (6%)
  between operations  0.67 us (2%)
    all_to_all x3, blocking collectives, exchange(): lax.all_to_all(blocks, axes, split_axis=0, concat_axis=0, axis_index_grou...  40.1 us
    pallas_call x3, Pallas kernels, call(): run(*[pltpu.with_memory_space_constraint(a, pltpu.VMEM) for a in args])  1.36 us
    pallas_call x1, Pallas kernels, on_device(): call(summary_kernel, [((BLOCKS, 6 * SHARE, LANES), F32), ((2 * SHARE, LAN...  1.25 us

profile of v4, /device:TPU:1, one launch (start us, length us, event | category | flops | bytes accessed | tf_op | source)
XLA Modules:
  0.0 43.5 jit_solution(13105721588612673913)
XLA Ops:
  0.6 1.2 %shard_map.109 = (f32[8,24,128]{2,1,0:T(8,128)S(1)}, f32[8,128]{1,0:T(8,128)S(1)}, f32[128,128]{1,0:T(8,128)S(1)}, f32[128,128]{1,0:T(8,128)S(1)}, bf16[128,128]...) custom-call(bf16[128,128]{1,0:T(8,128)(2,1)} %q_ref.1, ...), custom_call_target="tpu_custom_call" | custom-call | tf_op jit(solution)/shard_map/pallas_call | solution.py:211
  1.9 12.8 %all_to_all.15.in_ref = f32[8,24,128]{2,1,0:T(8,128)S(1)} all-to-all(f32[8,24,128]{2,1,0:T(8,128)S(1)} %get-tuple-element.21), channel_id=1, replica_groups={{40,32,56,48,8,0,24,16},{41,33,57,49,9,1,25,17},{42,34,58,50,10,2,26,18..., dimensions={0} | all-to-all | bytes 196608 | tf_op jit(solution)/shard_map/all_to_all | solution.py:205
  14.7 0.1 shard_map.110
  14.8 15.9 %all_to_all.16 = f16[8,24,128]{2,1,0:T(8,128)(2,1)S(1)} all-to-all(f16[8,24,128]{2,1,0:T(8,128)(2,1)S(1)} %convert_element_type.12), channel_id=1, replica_groups={{256,0,320,64,384,128,448,192},{257,1,321,65,385,129,449,193},{258,2,32..., dimensions={0} | all-to-all | bytes 98304 | tf_op jit(solution)/shard_map/all_to_all | solution.py:205
  30.7 0.1 shard_map.111
  30.8 11.5 %all_to_all.17 = f16[32,16,128]{2,1,0:T(8,128)(2,1)S(1)} all-to-all(f16[32,16,128]{2,1,0:T(8,128)(2,1)S(1)} %convert_element_type.14), channel_id=1, replica_groups={{13,5,29,21,12,4,28,20,15,7,31,23,14,6,30,22,9,1,25,17,8,0,24,16,11,3,2..., dimensions={0} | all-to-all | bytes 262144 | tf_op jit(solution)/shard_map/all_to_all | solution.py:205
  42.3 1.2 %shard_map.112 = (bf16[128,128]{1,0:T(8,128)(2,1)}, bf16[128,128]{1,0:T(8,128)(2,1)}, bf16[128,128]{1,0:T(8,128)(2,1)}, f32[16,128]{1,0:T(8,128)}, f32[16,128]{1,0:T(8,128)}, /*index=5*/f32[1,1]{1,0:T(1,128)}) custom-call(f32[32,16,128]{2,1,0:T(8,128)S(1)} %convert_element_type.15.back_ref, f32[128,128]{1,0:T(8,128)S(1)} %get-tuple-element.23.x_s, ...), custom_call_target="tpu_custom_call" | custom-call | tf_op jit(solution)/shard_map/pallas_call | solution.py:201
  (4 shorter events, 0.1 us)

commit v5 on v4

--- a/solution.py
+++ b/solution.py
@@ -15,7 +15,7 @@
 SHARE = MODES // GROUP
 CHANS = 8
 NEAR_FIRST = 5
-RING_ORDER = (4, 0, 5, 1, 6, 2, 7, 3)
+RING_ORDER = (5, 1, 4, 0, 6, 2, 7, 3)
 PLANE_FIRST = 21
 TOTAL = ROWS * BLOCKS * RING
 F32 = jnp.float32

time: 43.8 us -> 43.7 us (level)
  no operation moved by 1% of the time
where the time goes in v5:
time: 43.7 us; the launch traced here: 43.5 us
  blocking collectives  40.1 us (92%)
  Pallas kernels  2.61 us (6%)
  between operations  0.67 us (2%)
    all_to_all x3, blocking collectives, exchange(): lax.all_to_all(blocks, axes, split_axis=0, concat_axis=0, axis_index_grou...  40.1 us
    pallas_call x3, Pallas kernels, call(): run(*[pltpu.with_memory_space_constraint(a, pltpu.VMEM) for a in args])  1.36 us
    pallas_call x1, Pallas kernels, on_device(): call(summary_kernel, [((BLOCKS, 6 * SHARE, LANES), F32), ((2 * SHARE, LAN...  1.25 us

profile of v5, /device:TPU:1, one launch (start us, length us, event | category | flops | bytes accessed | tf_op | source)
XLA Modules:
  0.0 43.5 jit_solution(9351664367532674259)
XLA Ops:
  0.6 1.2 %shard_map.109 = (f32[8,24,128]{2,1,0:T(8,128)S(1)}, f32[8,128]{1,0:T(8,128)S(1)}, f32[128,128]{1,0:T(8,128)S(1)}, f32[128,128]{1,0:T(8,128)S(1)}, bf16[128,128]...) custom-call(bf16[128,128]{1,0:T(8,128)(2,1)} %q_ref.1, ...), custom_call_target="tpu_custom_call" | custom-call | tf_op jit(solution)/shard_map/pallas_call | solution.py:211
  1.9 12.8 %all_to_all.15.in_ref = f32[8,24,128]{2,1,0:T(8,128)S(1)} all-to-all(f32[8,24,128]{2,1,0:T(8,128)S(1)} %get-tuple-element.21), channel_id=1, replica_groups={{40,32,56,48,8,0,24,16},{41,33,57,49,9,1,25,17},{42,34,58,50,10,2,26,18..., dimensions={0} | all-to-all | bytes 196608 | tf_op jit(solution)/shard_map/all_to_all | solution.py:205
  14.7 0.1 shard_map.110
  14.8 15.3 %all_to_all.16 = f16[8,24,128]{2,1,0:T(8,128)(2,1)S(1)} all-to-all(f16[8,24,128]{2,1,0:T(8,128)(2,1)S(1)} %convert_element_type.12), channel_id=1, replica_groups={{320,64,256,0,384,128,448,192},{321,65,257,1,385,129,449,193},{322,66,2..., dimensions={0} | all-to-all | bytes 98304 | tf_op jit(solution)/shard_map/all_to_all | solution.py:205
  30.1 0.1 shard_map.111
  30.2 12.0 %all_to_all.17 = f16[32,16,128]{2,1,0:T(8,128)(2,1)S(1)} all-to-all(f16[32,16,128]{2,1,0:T(8,128)(2,1)S(1)} %convert_element_type.14), channel_id=1, replica_groups={{13,5,29,21,12,4,28,20,15,7,31,23,14,6,30,22,9,1,25,17,8,0,24,16,11,3,2..., dimensions={0} | all-to-all | bytes 262144 | tf_op jit(solution)/shard_map/all_to_all | solution.py:205
  42.3 1.2 %shard_map.112 = (bf16[128,128]{1,0:T(8,128)(2,1)}, bf16[128,128]{1,0:T(8,128)(2,1)}, bf16[128,128]{1,0:T(8,128)(2,1)}, f32[16,128]{1,0:T(8,128)}, f32[16,128]{1,0:T(8,128)}, /*index=5*/f32[1,1]{1,0:T(1,128)}) custom-call(f32[32,16,128]{2,1,0:T(8,128)S(1)} %convert_element_type.15.back_ref, f32[128,128]{1,0:T(8,128)S(1)} %get-tuple-element.23.x_s, ...), custom_call_target="tpu_custom_call" | custom-call | tf_op jit(solution)/shard_map/pallas_call | solution.py:201
  (4 shorter events, 0.1 us)
